TPU v7x, 32 devices: a whole 2x2x4 slice. The times are simulated.
32 devices in a mesh: context: 16 (over z, y, x), tensor: 2 (over core).
Axes of the slice: x: 2, y: 2, z: 4, core: 2. Of those that a mesh axis runs over, the one named last changes fastest.
Arguments:
- tokens: int32 [8192], P(('context', 'tensor')), may hold values from 0 to 511
- embedding: bfloat16 [512, 1920], replicated, may hold values from -6 to 6
- gain_a: float32 [1920], replicated, may hold values from 0.1 to 1.9
- in_proj_a: bfloat16 [3, 1920, 1920], P(None, 'tensor'), may hold values from -0.125 to 0.125
- short_a: float32 [3, 3, 1920], P(None, None, 'tensor'), may hold values from -4 to 4
- mr_filter: float32 [128, 1920], P(None, 'tensor'), may hold values from -0.5 to 0.5
- mr_skip: float32 [1920], P('tensor'), may hold values from -3 to 3
- out_proj_a: bfloat16 [1920, 1920], P('tensor'), may hold values from -0.125 to 0.125
- gain_b: float32 [1920], replicated, may hold values from 0.1 to 1.9
- in_proj_b: bfloat16 [3, 1920, 1920], P(None, 'tensor'), may hold values from -0.125 to 0.125
- short_b: float32 [3, 3, 1920], P(None, None, 'tensor'), may hold values from -4 to 4
- li_rate: float32 [16, 1920], P(None, 'tensor'), may hold values from 0 to 0.04, as said below
- li_residue: float32 [16, 1920], P(None, 'tensor'), may hold values from -1.5 to 1.5
- li_skip: float32 [1920], P('tensor'), may hold values from -3 to 3
- out_proj_b: bfloat16 [1920, 1920], P('tensor'), may hold values from -0.125 to 0.125
Outputs:
- hidden_out: bfloat16 [8192, 1920], P(('context', 'tensor'))
Inputs may be any that keep to these rules, and one draw needn't show every extreme that they name: `li_rate`: every rate lies between 0.05 / 8192 and 1 / 30 per position.
All inputs are finite; a program needn't handle non-finite values.
Results may differ from a plain program's by a relative error of at most 0.014.
Values may be sent and summed in bfloat16 or wider, within the bound.
A program may use at most 192 MiB of HBM per device.

v0:
```python
import functools

import jax
import jax.numpy as jnp
import numpy as np
from jax import lax
from jax.experimental import pallas as pl
from jax.experimental.pallas import tpu as pltpu
from jax.sharding import PartitionSpec as P

EPS = 1e-06
HALO = 160
LEAD = 16
BLOCK = 128
VMEM = 56 * 1024 * 1024
F32 = jnp.float32
BF16 = jnp.bfloat16


def params():
    return pltpu.CompilerParams(vmem_limit_bytes=VMEM)


def split(value):
    high = value.astype(BF16)
    return high, (value - high.astype(F32)).astype(BF16)


def np_split(value):
    high = value.astype(jnp.bfloat16)
    return high, (value - high.astype(np.float64)).astype(jnp.bfloat16)


def transforms():
    bins = np.concatenate([np.arange(0, BLOCK, 2), np.arange(1, BLOCK, 2)])
    angle = np.pi * (2 * bins[:, None] + 1) * np.arange(BLOCK)[None, :] / (2 * BLOCK)
    forward = np.concatenate([np.cos(angle), -np.sin(angle)], 0)
    inverse = forward.T / BLOCK
    fh, fl = np_split(forward)
    ih, il = np_split(inverse)
    return np.concatenate([fh, fl], 1), np.concatenate([ih, il], 1)


def dot(a, b):
    return jnp.dot(a, b, preferred_element_type=F32)


def dot_nt(a, b):
    return lax.dot_general(a, b, (((1,), (1,)), ((), ())), preferred_element_type=F32)


def normalize(rows, gain):
    wide = rows.astype(F32)
    inverse_rms = lax.rsqrt(jnp.mean(wide * wide, axis=1, keepdims=True) + EPS)
    return (wide * inverse_rms * gain).astype(BF16)


def forward_exact(fwd_ref, rows):
    return dot(fwd_ref[...], jnp.concatenate([rows, rows], 0))


def forward_wide(fwd_ref, rows):
    high, low = split(rows)
    return forward_exact(fwd_ref, high) + dot(fwd_ref[:, :BLOCK], low)


def inverse_wide(inv_ref, high_ref, low_ref):
    size = 2 * BLOCK
    return (
        dot(inv_ref[:, :size], high_ref[...])
        + dot(inv_ref[:, size:], high_ref[...])
        + dot(inv_ref[:, :size], low_ref[...])
    )


def onehot(tokens, vocab):
    return (tokens == lax.broadcasted_iota(jnp.int32, (tokens.shape[0], vocab), 1)).astype(BF16)


def short_filter(ref, part, row, count, taps):
    wide = ref[part, pl.ds(row, count + 8), :]
    return (
        taps[0] * wide[8:] + taps[1] * wide[7 : count + 7] + taps[2] * wide[6 : count + 6]
    )


def table_kernel(emb_ref, gain_ref, mat_ref, out_ref, normed):
    rows = emb_ref.shape[0]

    @pl.when(pl.program_id(0) == 0)
    def _():
        @pl.loop(0, rows // 32)
        def _(i):
            at = pl.ds(pl.multiple_of(i * 32, 32), 32)
            normed[at, :] = normalize(emb_ref[at, :], gain_ref[...])

    @pl.loop(0, rows // 256)
    def _(i):
        at = pl.ds(pl.multiple_of(i * 256, 256), 256)
        out_ref[0, at, :] = dot_nt(normed[at, :], mat_ref[0]).astype(BF16)


def make_table(embedding, gain, matrix):
    vocab, width = embedding.shape
    parts, channels, _ = matrix.shape
    return pl.pallas_call(
        table_kernel,
        grid=(parts,),
        in_specs=[
            pl.BlockSpec((vocab, width), lambda i: (0, 0)),
            pl.BlockSpec((1, width), lambda i: (0, 0)),
            pl.BlockSpec((1, channels, width), lambda i: (i, 0, 0)),
        ],
        out_specs=pl.BlockSpec((1, vocab, channels), lambda i: (i, 0, 0)),
        out_shape=jax.ShapeDtypeStruct((parts, vocab, channels), BF16),
        scratch_shapes=[pltpu.VMEM((vocab, width), BF16)],
        compiler_params=params(),
        cost_estimate=pl.CostEstimate(
            flops=2 * vocab * width * channels * parts,
            bytes_accessed=2 * parts * channels * (width + vocab),
            transcendentals=0,
        ),
    )(embedding, gain[None], matrix)


def medium_kernel(
    tok_ref, table_ref, taps_ref, filt_ref, skip_ref, fwd_ref, inv_ref, out_ref,
    proj, gate_f, gate_b, query, spec, freq, zh, zl,
):
    rows = tok_ref.shape[0]
    vocab = table_ref.shape[1]
    channels = table_ref.shape[2]
    length = rows - HALO
    for part in range(3):
        proj[part, 0:8, :] = jnp.zeros((8, channels), F32)
    third = rows // 3
    for i in range(3):
        picked = onehot(tok_ref[i * third : (i + 1) * third, :], vocab)
        for part in range(3):
            proj[part, 8 + i * third : 8 + (i + 1) * third, :] = dot(picked, table_ref[part])

    @pl.loop(0, rows // 32)
    def _(i):
        row = pl.multiple_of(i * 32, 32)
        taps = [[taps_ref[j, pl.ds(part, 1), :] for j in range(3)] for part in range(3)]
        query[pl.ds(row, 32), :] = short_filter(proj, 0, row, 32, taps[0])
        gate = (
            short_filter(proj, 1, row, 32, taps[1]) * short_filter(proj, 2, row, 32, taps[2])
        ).astype(BF16)
        gate_b[pl.ds(row, 32), :] = gate
        gate_f[pl.ds(row, 32), :] = gate.astype(F32)

    filt = filt_ref[...]
    freq[...] = forward_wide(fwd_ref, filt)
    order = lax.broadcasted_iota(jnp.int32, (BLOCK, BLOCK), 0) + lax.broadcasted_iota(
        jnp.int32, (BLOCK, BLOCK), 1
    )
    flip = (order == BLOCK - 1).astype(BF16)
    high, low = split(filt)
    backward = dot(flip, high) + dot(flip, low)
    last = jnp.sum(backward * gate_f[HALO - BLOCK : HALO, :], axis=0, keepdims=True)
    prior = jnp.sum(backward * gate_f[HALO - BLOCK - 1 : HALO - 1, :], axis=0, keepdims=True)
    at = lax.broadcasted_iota(jnp.int32, (LEAD, channels), 0)
    summed = jnp.where(at == LEAD - 1, last, jnp.where(at == LEAD - 2, prior, 0.0))
    edge = slice(HALO - LEAD, HALO)
    out_ref[0:LEAD, :] = jnp.where(
        at >= LEAD - 2, query[edge, :] * (summed + skip_ref[...] * gate_f[edge, :]), 0.0
    ).astype(BF16)

    spec[0] = forward_exact(fwd_ref, gate_b[HALO - BLOCK : HALO, :])
    for b in range(length // BLOCK):
        start = HALO + b * BLOCK
        now, old = (b + 1) % 2, b % 2
        spec[now] = forward_exact(fwd_ref, gate_b[start : start + BLOCK, :])
        for half, sign in ((0, 1.0), (1, -1.0)):

            @pl.loop(0, BLOCK // 64)
            def _(i):
                re = pl.ds(pl.multiple_of(half * (BLOCK // 2) + i * 32, 32), 32)
                im = pl.ds(pl.multiple_of(BLOCK + half * (BLOCK // 2) + i * 32, 32), 32)
                u = spec[now, re, :] - sign * spec[old, im, :]
                v = spec[now, im, :] + sign * spec[old, re, :]
                a, c = freq[re, :], freq[im, :]
                zh[re, :], zl[re, :] = split(u * a - v * c)
                zh[im, :], zl[im, :] = split(u * c + v * a)

        here = slice(start, start + BLOCK)
        conv = inverse_wide(inv_ref, zh, zl)
        out_ref[start - HALO + LEAD : start - HALO + LEAD + BLOCK, :] = (
            query[here, :] * (conv + skip_ref[...] * gate_f[here, :])
        ).astype(BF16)


def medium_mix(tokens, table, taps, filt, skip, fwd, inv):
    rows = tokens.shape[0]
    channels = table.shape[2]
    return pl.pallas_call(
        medium_kernel,
        out_shape=jax.ShapeDtypeStruct((rows - HALO + LEAD, channels), BF16),
        scratch_shapes=[
            pltpu.VMEM((3, rows + 8, channels), F32),
            pltpu.VMEM((rows, channels), F32),
            pltpu.VMEM((rows, channels), BF16),
            pltpu.VMEM((rows, channels), F32),
            pltpu.VMEM((2, 2 * BLOCK, channels), F32),
            pltpu.VMEM((2 * BLOCK, channels), F32),
            pltpu.VMEM((2 * BLOCK, channels), BF16),
            pltpu.VMEM((2 * BLOCK, channels), BF16),
        ],
        compiler_params=params(),
    )(tokens[:, None], table, taps, filt, skip[None], fwd, inv)


def second_kernel(
    tok_ref, emb_ref, mix_ref, out_ref_w, gain_ref, mat_ref, taps_ref, rate_ref,
    second_ref, query_ref, gate_ref, before_ref, closing_ref,
    acc, normed, proj, gate_f,
):
    step = pl.program_id(0)
    rows, width = acc.shape
    vocab = emb_ref.shape[0]
    length = rows - LEAD
    channels = mat_ref.shape[1]
    tile = rows // 3

    @pl.when(step == 0)
    def _():
        @pl.loop(0, 3)
        def _(i):
            at = pl.ds(pl.multiple_of(i * tile, 16), tile)
            picked = onehot(tok_ref[at, :], vocab)
            acc[at, :] = dot(picked, emb_ref[...]) + dot(mix_ref[0, at, :], out_ref_w[0])

    @pl.when(step == 1)
    def _():
        @pl.loop(0, 3)
        def _(i):
            at = pl.ds(pl.multiple_of(i * tile, 16), tile)
            acc[at, :] = acc[at, :] + dot(mix_ref[0, at, :], out_ref_w[0])

        @pl.loop(0, rows // 16)
        def _(i):
            at = pl.ds(pl.multiple_of(i * 16, 16), 16)
            row = acc[at, :].astype(BF16)
            second_ref[at, :] = row
            normed[at, :] = normalize(row, gain_ref[...])

    for stage, part in ((1, 1), (2, 2), (3, 0)):

        @pl.when(step == stage)
        def _():
            @pl.loop(0, 3)
            def _(i):
                at = pl.ds(pl.multiple_of(i * tile, 16), tile)
                proj[part, at, :] = (
                    dot_nt(normed[at, :], mat_ref[0]).astype(BF16).astype(F32)
                )

    @pl.when(step == 2)
    def _():
        taps = [[taps_ref[j, pl.ds(part, 1), :] for j in range(3)] for part in range(3)]

        @pl.loop(0, length // 32)
        def _(i):
            row = pl.multiple_of(i * 32, 32)
            at = pl.multiple_of(row + LEAD - 8, 8)
            gate = (
                short_filter(proj, 1, at, 32, taps[1]) * short_filter(proj, 2, at, 32, taps[2])
            ).astype(BF16)
            gate_ref[pl.ds(row, 32), :] = gate
            gate_f[pl.ds(row, 32), :] = gate.astype(F32)

        decay = jnp.exp(-rate_ref[...])
        state = jnp.zeros(decay.shape, F32)
        for b in range(length // BLOCK):
            before_ref[b] = state

            def advance(i, state):
                tile8 = gate_f[pl.ds(pl.multiple_of(b * BLOCK + i * 8, 8), 8), :]
                for r in range(8):
                    state = state * decay + tile8[r : r + 1, :]
                return state

            state = lax.fori_loop(0, BLOCK // 8, advance, state)
        closing_ref[...] = state.astype(BF16)

    @pl.when(step == 3)
    def _():
        taps = [taps_ref[j, pl.ds(0, 1), :] for j in range(3)]

        @pl.loop(0, length // 32)
        def _(i):
            row = pl.multiple_of(i * 32, 32)
            at = pl.multiple_of(row + LEAD - 8, 8)
            query_ref[pl.ds(row, 32), :] = short_filter(proj, 0, at, 32, taps)


def second_block(tokens, embedding, mixes, weights, gain, matrix, taps, rate):
    _, rows, channels = mixes.shape
    vocab, width = embedding.shape
    length = rows - LEAD
    modes = rate.shape[0]
    whole2 = lambda i: (0, 0)
    whole3 = lambda i: (0, 0, 0)
    return pl.pallas_call(
        second_kernel,
        grid=(4,),
        in_specs=[
            pl.BlockSpec((rows, 1), whole2),
            pl.BlockSpec((vocab, width), whole2),
            pl.BlockSpec((1, rows, channels), lambda i: (jnp.minimum(i, 1), 0, 0)),
            pl.BlockSpec((1, channels, width), lambda i: (jnp.minimum(i, 1), 0, 0)),
            pl.BlockSpec((1, width), whole2),
            pl.BlockSpec(
                (1, channels, width),
                lambda i: (jnp.where(i == 3, 0, jnp.where(i == 2, 2, 1)), 0, 0),
            ),
            pl.BlockSpec(taps.shape, whole3),
            pl.BlockSpec(rate.shape, whole2),
        ],
        out_specs=[
            pl.BlockSpec((rows, width), whole2),
            pl.BlockSpec((length, channels), whole2),
            pl.BlockSpec((length, channels), whole2),
            pl.BlockSpec((length // BLOCK, modes, channels), whole3),
            pl.BlockSpec((modes, channels), whole2),
        ],
        out_shape=[
            jax.ShapeDtypeStruct((rows, width), BF16),
            jax.ShapeDtypeStruct((length, channels), F32),
            jax.ShapeDtypeStruct((length, channels), BF16),
            jax.ShapeDtypeStruct((length // BLOCK, modes, channels), F32),
            jax.ShapeDtypeStruct((modes, channels), BF16),
        ],
        scratch_shapes=[
            pltpu.VMEM((rows, width), F32),
            pltpu.VMEM((rows, width), BF16),
            pltpu.VMEM((3, rows, channels), F32),
            pltpu.VMEM((length, channels), F32),
        ],
        compiler_params=params(),
    )(tokens[:, None], embedding, mixes, weights, gain[None], matrix, taps, rate)


def lanes(channels):
    return [(at, min(128, channels - at)) for at in range(0, channels, 128)]


def modal_rows(rate_ref, coef_ref, groups, lane, width, store):
    modes = rate_ref.shape[0]
    at = lax.broadcasted_iota(jnp.int32, (8, width), 0).astype(F32)
    cols = slice(lane, lane + width)
    values, steps = [], []
    for m in range(modes):
        rate = rate_ref[m : m + 1, cols]
        values.append(coef_ref[m : m + 1, cols] * jnp.exp(-rate * at))
        steps.append(jnp.broadcast_to(jnp.exp(-8.0 * rate), (8, width)))

    def advance(group, values):
        terms = list(values)
        while len(terms) > 1:
            terms = [a + b for a, b in zip(terms[::2], terms[1::2])] + (
                [terms[-1]] if len(terms) % 2 else []
            )
        store(group, terms[0])
        return [v * s for v, s in zip(values, steps)]

    lax.fori_loop(0, groups, advance, values)


def within_kernel(gate_ref, rate_ref, res_ref, skip_ref, fwd_ref, inv_ref, out_ref,
                  coef, taps, freq, spec, zh, zl):
    length, channels = gate_ref.shape
    rate = rate_ref[...]
    doubled = 2.0 * rate
    series = doubled * (1.0 - doubled * (0.5 - doubled * (1.0 / 6.0 - doubled * (1.0 / 24.0 - doubled / 120.0))))
    coef[...] = res_ref[...] * jnp.sqrt(
        jnp.where(doubled < 0.03, series, 1.0 - jnp.exp(-doubled))
    )
    for lane, width in lanes(channels):

        def store(group, rows):
            taps[pl.ds(pl.multiple_of(group * 8, 8), 8), lane : lane + width] = rows

        modal_rows(rate_ref, coef, BLOCK // 8, lane, width, store)
    freq[...] = forward_wide(fwd_ref, taps[...])
    for b in range(length // BLOCK):
        here = slice(b * BLOCK, (b + 1) * BLOCK)
        spec[...] = forward_exact(fwd_ref, gate_ref[here, :])

        @pl.loop(0, BLOCK // 32)
        def _(i):
            re = pl.ds(pl.multiple_of(i * 32, 32), 32)
            im = pl.ds(pl.multiple_of(BLOCK + i * 32, 32), 32)
            u, v = spec[re, :], spec[im, :]
            a, c = freq[re, :], freq[im, :]
            zh[re, :], zl[re, :] = split(u * a - v * c)
            zh[im, :], zl[im, :] = split(u * c + v * a)

        out_ref[here, :] = inverse_wide(inv_ref, zh, zl) + skip_ref[...] * gate_ref[
            here, :
        ].astype(F32)


def within_block(gate, rate, residue, skip, fwd, inv):
    length, channels = gate.shape
    return pl.pallas_call(
        within_kernel,
        out_shape=jax.ShapeDtypeStruct((length, channels), F32),
        scratch_shapes=[
            pltpu.VMEM(rate.shape, F32),
            pltpu.VMEM((BLOCK, channels), F32),
            pltpu.VMEM((2 * BLOCK, channels), F32),
            pltpu.VMEM((2 * BLOCK, channels), F32),
            pltpu.VMEM((2 * BLOCK, channels), BF16),
            pltpu.VMEM((2 * BLOCK, channels), BF16),
        ],
        compiler_params=params(),
        cost_estimate=pl.CostEstimate(
            flops=8_000_000_000, bytes_accessed=4_000_000, transcendentals=0
        ),
    )(gate, rate, residue, skip[None], fwd, inv)


def finish_kernel(pos_ref, seg_ref, rate_ref, res_ref, before_ref, query_ref, within_ref,
                  out_ref, coef):
    length, channels = query_ref.shape
    rate = rate_ref[...]
    shard_step = jnp.exp(-rate * float(length))
    position = pos_ref[0]

    def gather(source, total):
        return jnp.where(
            source < position, total * shard_step + seg_ref[source].astype(F32), total
        )

    incoming = lax.fori_loop(0, seg_ref.shape[0], gather, jnp.zeros(rate.shape, F32))
    doubled = 2.0 * rate
    series = doubled * (1.0 - doubled * (0.5 - doubled * (1.0 / 6.0 - doubled * (1.0 / 24.0 - doubled / 120.0))))
    gain = res_ref[...] * jnp.sqrt(jnp.where(doubled < 0.03, series, 1.0 - jnp.exp(-doubled)))
    for b in range(length // BLOCK):
        coef[b] = (
            gain * jnp.exp(-rate) * (before_ref[b] + jnp.exp(-rate * float(b * BLOCK)) * incoming)
        )
    for b in range(length // BLOCK):
        for lane, width in lanes(channels):
            cols = slice(lane, lane + width)

            def store(group, rows):
                at = pl.ds(pl.multiple_of(b * BLOCK + group * 8, 8), 8)
                out_ref[at, cols] = query_ref[at, cols] * (within_ref[at, cols] + rows)

            modal_rows(rate_ref, coef.at[b], BLOCK // 8, lane, width, store)


def finish_block(position, segments, rate, residue, before, query, within):
    length, channels = query.shape
    return pl.pallas_call(
        finish_kernel,
        in_specs=[pl.BlockSpec(memory_space=pltpu.SMEM)]
        + [pl.BlockSpec(memory_space=pltpu.VMEM)] * 6,
        out_specs=pl.BlockSpec(memory_space=pltpu.VMEM),
        out_shape=jax.ShapeDtypeStruct((length, channels), F32),
        scratch_shapes=[pltpu.VMEM(before.shape, F32)],
        compiler_params=params(),
    )(position, segments, rate, residue, before, query, within)


def on_device(
    tokens, embedding, gain_a, in_proj_a, short_a, mr_filter, mr_skip, out_proj_a,
    gain_b, in_proj_b, short_b, li_rate, li_residue, li_skip, out_proj_b,
):
    fwd, inv = [jnp.asarray(m) for m in transforms()]
    own_rows = tokens.shape[0]
    length = own_rows * lax.axis_size("tensor")
    position = lax.axis_index("context")
    side = lax.axis_index("tensor")
    swap = [(0, 1), (1, 0)]
    all_tokens = lax.all_gather(tokens, ("context", "tensor"), axis=0, tiled=True)
    weights_a = lax.all_gather(out_proj_a, "tensor", axis=0)
    weights_b = lax.ppermute(out_proj_b, "tensor", swap)
    table = make_table(embedding, gain_a, in_proj_a)
    padded = jnp.concatenate([jnp.full((HALO,), -1, jnp.int32), all_tokens])
    near = lax.dynamic_slice_in_dim(padded, position * length, length + HALO, 0)
    mixed = medium_mix(near, table, short_a, mr_filter, mr_skip, fwd, inv)
    mixes = lax.all_gather(mixed, "tensor", axis=0)
    second, query, gate, before, closing = second_block(
        near[HALO - LEAD :], embedding, mixes, weights_a, gain_b, in_proj_b, short_b, li_rate
    )
    segments = lax.all_gather(closing, "context", axis=0)
    within = within_block(gate, li_rate, li_residue, li_skip, fwd, inv)
    mixture = finish_block(
        position[None], segments, li_rate, li_residue, before, query, within
    ).astype(BF16)
    sent = lax.dynamic_slice_in_dim(mixture, (1 - side) * own_rows, own_rows, 0)
    kept = lax.dynamic_slice_in_dim(mixture, side * own_rows, own_rows, 0)
    other = lax.ppermute(sent, "tensor", swap)
    residual = lax.dynamic_slice_in_dim(second, LEAD + side * own_rows, own_rows, 0)
    summed = residual.astype(F32) + dot(kept, out_proj_b)
    return (summed + dot(other, weights_b)).astype(BF16)


def solution(mesh):
    return jax.shard_map(
        on_device,
        mesh=mesh,
        in_specs=(
            P(("context", "tensor")),
            P(),
            P(),
            P(None, "tensor", None),
            P(None, None, "tensor"),
            P(None, "tensor"),
            P("tensor"),
            P("tensor", None),
            P(),
            P(None, "tensor", None),
            P(None, None, "tensor"),
            P(None, "tensor"),
            P(None, "tensor"),
            P("tensor"),
            P("tensor", None),
        ),
        out_specs=P(("context", "tensor"), None),
        check_vma=False,
    )
```

profile of v0, /device:TPU:1, one launch (start us, length us, event | category | flops | bytes accessed | tf_op | source)
XLA Modules:
  0.0 223.1 jit_solution(176757365351982683)
XLA Ops:
  6.5 0.0 all-gather.7.cloned.1.call-start
  6.5 43.4 %all-gather.3 = s32[32,1,256]{2,1,0:T(1,128)S(1)} all-gather(s32[1,1,256]{2,1,0:T(1,128)} %bitcast.16), channel_id=1, replica_groups=mesh['context'=16,'tensor'=2] {'context','tensor'}, dimensions={0}, use_global_device_ids=true | all-gather | bytes 33792 | tf_op jit(solution)/shard_map/all_gather | solution.py:479
  49.9 0.1 pad_dynamic-slice_fusion
  50.0 0.9 broadcast_in_dim.30.tok_ref
  50.8 1.3 broadcast_in_dim.24.gain_ref
  52.1 2.0 copy.23.filt_ref
  54.2 13.4 %shard_map.163.table_ref = bf16[3,512,960]{2,1,0:T(8,128)(2,1)} custom-call(bf16[512,1920]{1,0:T(8,128)(2,1)} %emb_ref.3, f32[1,1920]{1,0:T(1,128)} %broadcast_in_dim.24.gain_ref, bf16[3,960,1920]{2,1,0:T(8,128)(2,1)} %mat_ref.2), custom_call_target="tpu_custom_call" | custom-call | flops 5662310400 | bytes 14008320 | tf_op jit(solution)/shard_map/pallas_call | solution.py:106
  67.6 13.0 %shard_map.164 = bf16[528,960]{1,0:T(8,128)(2,1)} custom-call(s32[672,1]{1,0:T(8,128)} %broadcast_in_dim.30.tok_ref, bf16[3,512,960]{2,1,0:T(8,128)(2,1)} %shard_map.163.table_ref, f32[3,3,960]{2,1,0:T(4,128)} %taps_ref.2, f32[128,960]{1,0:T(8,128)} %copy.23.filt_ref, f32[1,960]{1,0:T(1,128)} %bitcast.15, bf16[256,256]{1,0:T(8,128)(2,1)} %constant.29.clone.fwd_ref, ...), custom_call_target="tpu_custom_call" | custom-call | tf_op jit(solution)/shard_map/pallas_call | solution.py:197
  80.6 0.0 all-gather.7.cloned.1.call-update
  80.7 0.0 copy-start
  80.7 0.0 all-gather.9.cloned.1.call-start
  80.7 0.7 all-gather.9.cloned.1.call-update
  81.4 0.3 collective-permute-start.1
  81.7 0.1 slice.3
  81.8 0.8 broadcast_in_dim.29.tok_ref
  82.6 0.0 copy-done
  82.6 0.6 broadcast_in_dim.26.gain_ref
  83.2 6.4 %all-gather.7.cloned.1.call-done = bf16[1056,960]{1,0:T(8,128)(2,1)} async-done(((bf16[528,960]{1,0:T(8,128)(2,1)}), bf16[1056,960]{1,0:T(8,128)(2,1)}) %all-gather.7.cloned.1.call-update) | async-done | bytes 2027536 | tf_op jit(solution)/shard_map/all_gather | solution.py:486
  89.6 18.9 %all-gather.9.cloned.1.call-done = bf16[1920,1920]{1,0:T(8,128)(2,1)} async-done(((bf16[960,1920]{1,0:T(8,128)(2,1)}), bf16[1920,1920]{1,0:T(8,128)(2,1)}) %all-gather.9.cloned.1.call-update) | async-done | bytes 7372816 | tf_op jit(solution)/shard_map/all_gather | solution.py:480
  108.6 35.0 %shard_map.165 = (bf16[528,1920]{1,0:T(8,128)(2,1)}, f32[512,960]{1,0:T(8,128)}, bf16[512,960]{1,0:T(8,128)(2,1)}, f32[4,16,960]{2,1,0:T(8,128)}, bf16[16,960]{1,0:T(8,128)(2,1)}) custom-call(s32[528,1]{1,0:T(8,128)} %broadcast_in_dim.29.tok_ref, bf16[512,1920]{1,0:T(8,128)(2,1)} %emb_ref.3, bf16[2,528,960]{2,1,0:T(8,128)(2,1)} %bitcast.12, ...), custom_call_target="tpu_custom_call" | custom-call | tf_op jit(solution)/shard_map/pallas_call | solution.py:305
  143.6 39.2 %all-gather.2 = bf16[256,960]{1,0:T(8,128)(2,1)} all-gather(bf16[16,960]{1,0:T(8,128)(2,1)} %get-tuple-element.11), channel_id=4, replica_groups=mesh['context'=16,'tensor'=2] {'context'}, dimensions={0}, use_global_device_ids=true | all-gather | bytes 522240 | tf_op jit(solution)/shard_map/all_gather | solution.py:490
  182.9 7.2 %shard_map.166.within_ref = f32[512,960]{1,0:T(8,128)} custom-call(bf16[512,960]{1,0:T(8,128)(2,1)} %get-tuple-element.14.gate_ref, f32[16,960]{1,0:T(8,128)} %rate_ref.5, f32[16,960]{1,0:T(8,128)} %res_ref.3, f32[1,960]{1,0:T(1,128)} %bitcast.17, bf16[256,256]{1,0:T(8,128)(2,1)} %constant.29.clone.fwd_ref, bf16[128,512]{1,0:T(8,128)(2,1)} %constant.30.clone.inv_ref), custom_call_target="tpu_custom_call" | custom-call | flops 8000000000 | bytes 4000000 | tf_op jit(solution)/shard_map/pallas_call | solution.py:407
  190.1 9.0 %shard_map.167 = f32[512,960]{1,0:T(8,128)} custom-call(s32[1]{0:T(128)} %bitcast.5.pos_ref, bf16[16,16,960]{2,1,0:T(8,128)(2,1)} %bitcast.13, f32[16,960]{1,0:T(8,128)} %rate_ref.5, f32[16,960]{1,0:T(8,128)} %res_ref.3, f32[4,16,960]{2,1,0:T(8,128)} %get-tuple-element.12.before_ref, f32[512,960]{1,0:T(8,128)} %get-tuple-element.13.query_ref, ...), custom_call_target="tpu_custom_call" | custom-call | tf_op jit(solution)/shard_map/pallas_call | solution.py:458
  199.0 1.7 convert_element_type.10
  200.8 7.5 %collective-permute-start = (bf16[256,960]{1,0:T(8,128)(2,1)S(1)}, bf16[256,960]{1,0:T(8,128)(2,1)S(1)}, u32[]{:S(2)}, u32[]{:S(2)}) collective-permute-start(bf16[256,960]{1,0:T(8,128)(2,1)S(1)} %constant_dynamic-slice_fusion), channel_id=1, source_target_pairs={{0,1},{1,0},{2,3},{3,2},{4,5},{5,4},{6,7},{7,6},{8,9},{9,8},{10,11... | collective-permute-start | bytes 1474568 | tf_op jit(solution)/shard_map/ppermute | solution.py:497
  208.4 3.6 %convolution_add_fusion.1 = f32[256,1920]{1,0:T(8,128)S(1)} fusion(bf16[960,1920]{1,0:T(8,128)(2,1)} %param.31, bf16[528,1920]{1,0:T(8,128)(2,1)} %get-tuple-element.10, s32[]{:T(128)S(6)} %select_n.13, bf16[512,960]{1,0:T(8,128)(2,1)S(1)} %convert_element_type.10, s32[]{:T(128)S(6)} %select_n.14), kind=kOutput, calls=%fused_computation.1 | convolution fusion | flops 944701440 | bytes 7159816 | tf_op jit(solution)/shard_map/dot_general | solution.py:45
  211.9 0.0 collective-permute-done.1
  211.9 0.0 collective-permute-done
  211.9 4.3 %fusion = bf16[256,1920]{1,0:T(8,128)(2,1)} fusion(f32[256,1920]{1,0:T(8,128)S(1)} %convolution_add_fusion.1, bf16[256,960]{1,0:T(8,128)(2,1)S(1)} %collective-permute-done, bf16[960,1920]{1,0:T(8,128)(2,1)} %collective-permute-done.1), kind=kOutput, calls=%fused_computation.2 | convolution fusion | flops 944701440 | bytes 7127040 | tf_op jit(solution)/shard_map/dot_general | solution.py:45
  (1 shorter events, 0.0 us)
Async XLA Ops:
  6.5 83.1 %all-gather.7.cloned.1.call-start = ((), (), s32[]{:S(2)}) async-start(), calls=%async_computation | async-start | bytes 3244032 | tf_op jit(solution)/shard_map/all_gather | solution.py:486
  80.7 1.9 copy-start
  80.7 27.9 %all-gather.9.cloned.1.call-start = ((), (), s32[]{:S(2)}) async-start(), calls=%async_computation.1 | async-start | bytes 11059200 | tf_op jit(solution)/shard_map/all_gather | solution.py:480
  81.4 130.5 %collective-permute-start.1 = (bf16[960,1920]{1,0:T(8,128)(2,1)}, bf16[960,1920]{1,0:T(8,128)(2,1)}, u32[]{:S(2)}, u32[]{:S(2)}) collective-permute-start(bf16[960,1920]{1,0:T(8,128)(2,1)} %param.31), channel_id=1, source_target_pairs={{0,1},{1,0},{2,3},{3,2},{4,5},{5,4},{6,7},{7,6},{8,9},{9,8},{10,11... | collective-permute-start | bytes 11059208 | tf_op jit(solution)/shard_map/ppermute | solution.py:481
  200.8 11.1 %collective-permute-start = (bf16[256,960]{1,0:T(8,128)(2,1)S(1)}, bf16[256,960]{1,0:T(8,128)(2,1)S(1)}, u32[]{:S(2)}, u32[]{:S(2)}) collective-permute-start(bf16[256,960]{1,0:T(8,128)(2,1)S(1)} %constant_dynamic-slice_fusion), channel_id=1, source_target_pairs={{0,1},{1,0},{2,3},{3,2},{4,5},{5,4},{6,7},{7,6},{8,9},{9,8},{10,11... | collective-permute-start | bytes 1474568 | tf_op jit(solution)/shard_map/ppermute | solution.py:497
Sparse Core Ops, SparseCore 0:
  80.8 8.7 all-gather.6
  91.2 17.3 all-gather.8
where the time goes:
time: 223 us
  blocking collectives  82.6 us (37%)
  Pallas kernels  77.7 us (35%)
  waiting for transfers between devices  26.1 us (12%)
  between operations  13.5 us (6%)
  starting transfers between devices  7.83 us (4%)
  matrix products  7.83 us (4%)
  local copies, waits for them, and re-layouts  5.85 us (3%)
    all_gather x1, blocking collectives, on_device(): lax.all_gather(tokens, ('context', 'tensor'), axis=0, tiled=True)  43.4 us
    all_gather x1, blocking collectives, on_device(): segments = lax.all_gather(closing, 'context', axis=0)  39.2 us
    pallas_call x1, Pallas kernels, second_block(): pl.pallas_call(second_kernel, grid=(4,), in_specs=[pl.BlockSpec((rows, 1)...  35 us
    all_gather x1, waiting for transfers between devices, on_device(): weights_a = lax.all_gather(out_proj_a, 'tensor', axis=0)  18.9 us
    pallas_call x1, Pallas kernels, make_table(): pl.pallas_call(table_kernel, grid=(parts,), in_specs=[pl.BlockSpec((vocab...  13.4 us
    pallas_call x1, Pallas kernels, medium_mix(): pl.pallas_call(medium_kernel, out_shape=jax.ShapeDtypeStruct((rows - HALO...  13 us
    pallas_call x1, Pallas kernels, finish_block(): pl.pallas_call(finish_kernel, in_specs=[pl.BlockSpec(memory_space=pltpu.S...  8.96 us
    dot_general x2, matrix products, dot(): return jnp.dot(a, b, preferred_element_type=F32)  7.83 us
  transfers between devices with their start and end apart: 4, of which 2 were waited for; matrix products, arithmetic and copies ran while one was open for 3% of the time, Pallas kernels for 23%

commit v1 on v0

--- a/solution.py
+++ b/solution.py
@@ -17,8 +17,19 @@
 BF16 = jnp.bfloat16
 
 
-def params():
-    return pltpu.CompilerParams(vmem_limit_bytes=VMEM)
+MESH = pl.DeviceIdType.MESH
+
+
+def params(collective=None):
+    if collective is None:
+        return pltpu.CompilerParams(vmem_limit_bytes=VMEM)
+    return pltpu.CompilerParams(
+        vmem_limit_bytes=VMEM, collective_id=collective, has_side_effects=True
+    )
+
+
+def chunks(total, size=256):
+    return [slice(at, min(at + size, total)) for at in range(0, total, size)]
 
 
 def split(value):
@@ -94,10 +105,8 @@
             at = pl.ds(pl.multiple_of(i * 32, 32), 32)
             normed[at, :] = normalize(emb_ref[at, :], gain_ref[...])
 
-    @pl.loop(0, rows // 256)
-    def _(i):
-        at = pl.ds(pl.multiple_of(i * 256, 256), 256)
-        out_ref[0, at, :] = dot_nt(normed[at, :], mat_ref[0]).astype(BF16)
+    for cols in chunks(mat_ref.shape[1]):
+        out_ref[0, :, cols] = dot_nt(normed[...], mat_ref[0, cols, :]).astype(BF16)
 
 
 def make_table(embedding, gain, matrix):
@@ -124,9 +133,12 @@
 
 
 def medium_kernel(
-    tok_ref, table_ref, taps_ref, filt_ref, skip_ref, fwd_ref, inv_ref, out_ref,
-    proj, gate_f, gate_b, query, spec, freq, zh, zl,
+    tok_ref, table_ref, taps_ref, filt_ref, skip_ref, fwd_ref, inv_ref, out_ref, peer_ref,
+    proj, gate_f, gate_b, query, spec, freq, zh, zl, inbox, send_sem, recv_sem,
 ):
+    peer = 1 - lax.axis_index("tensor")
+    barrier = pltpu.get_barrier_semaphore()
+    pl.semaphore_signal(barrier, inc=1, device_id={"tensor": peer}, device_id_type=MESH)
     rows = tok_ref.shape[0]
     vocab = table_ref.shape[1]
     channels = table_ref.shape[2]
@@ -167,6 +179,8 @@
         at >= LEAD - 2, query[edge, :] * (summed + skip_ref[...] * gate_f[edge, :]), 0.0
     ).astype(BF16)
 
+    pl.semaphore_wait(barrier, 1)
+    copies = []
     spec[0] = forward_exact(fwd_ref, gate_b[HALO - BLOCK : HALO, :])
     for b in range(length // BLOCK):
         start = HALO + b * BLOCK
@@ -189,6 +203,21 @@
         out_ref[start - HALO + LEAD : start - HALO + LEAD + BLOCK, :] = (
             query[here, :] * (conv + skip_ref[...] * gate_f[here, :])
         ).astype(BF16)
+        first = 0 if b == 0 else LEAD + b * BLOCK
+        part = pl.ds(first, LEAD + (b + 1) * BLOCK - first)
+        copy = pltpu.make_async_remote_copy(
+            src_ref=out_ref.at[part],
+            dst_ref=inbox.at[part],
+            send_sem=send_sem.at[b],
+            recv_sem=recv_sem.at[b],
+            device_id={"tensor": peer},
+            device_id_type=MESH,
+        )
+        copy.start()
+        copies.append(copy)
+    for copy in copies:
+        copy.wait()
+    peer_ref[...] = inbox[...]
 
 
 def medium_mix(tokens, table, taps, filt, skip, fwd, inv):
@@ -196,7 +225,7 @@
     channels = table.shape[2]
     return pl.pallas_call(
         medium_kernel,
-        out_shape=jax.ShapeDtypeStruct((rows - HALO + LEAD, channels), BF16),
+        out_shape=[jax.ShapeDtypeStruct((rows - HALO + LEAD, channels), BF16)] * 2,
         scratch_shapes=[
             pltpu.VMEM((3, rows + 8, channels), F32),
             pltpu.VMEM((rows, channels), F32),
@@ -206,37 +235,38 @@
             pltpu.VMEM((2 * BLOCK, channels), F32),
             pltpu.VMEM((2 * BLOCK, channels), BF16),
             pltpu.VMEM((2 * BLOCK, channels), BF16),
-        ],
-        compiler_params=params(),
+            pltpu.VMEM((rows - HALO + LEAD, channels), BF16),
+            pltpu.SemaphoreType.DMA(((rows - HALO) // BLOCK,)),
+            pltpu.SemaphoreType.DMA(((rows - HALO) // BLOCK,)),
+        ],
+        compiler_params=params(0),
     )(tokens[:, None], table, taps, filt, skip[None], fwd, inv)
 
 
 def second_kernel(
-    tok_ref, emb_ref, mix_ref, out_ref_w, gain_ref, mat_ref, taps_ref, rate_ref,
+    tok_ref, emb_ref, mix_ref, peer_ref, own_w, peer_w, gain_ref, mat_ref, taps_ref, rate_ref,
     second_ref, query_ref, gate_ref, before_ref, closing_ref,
-    acc, normed, proj, gate_f,
+    acc, normed, proj, gate_f, weight, weight_sem,
 ):
     step = pl.program_id(0)
     rows, width = acc.shape
     vocab = emb_ref.shape[0]
     length = rows - LEAD
     channels = mat_ref.shape[1]
-    tile = rows // 3
+    fetch = pltpu.make_async_copy(peer_w, weight, weight_sem)
 
     @pl.when(step == 0)
     def _():
-        @pl.loop(0, 3)
-        def _(i):
-            at = pl.ds(pl.multiple_of(i * tile, 16), tile)
-            picked = onehot(tok_ref[at, :], vocab)
-            acc[at, :] = dot(picked, emb_ref[...]) + dot(mix_ref[0, at, :], out_ref_w[0])
+        fetch.start()
+        picked = onehot(tok_ref[...], vocab)
+        for cols in chunks(width, 384):
+            acc[:, cols] = dot(picked, emb_ref[:, cols]) + dot(mix_ref[...], own_w[:, cols])
 
     @pl.when(step == 1)
     def _():
-        @pl.loop(0, 3)
-        def _(i):
-            at = pl.ds(pl.multiple_of(i * tile, 16), tile)
-            acc[at, :] = acc[at, :] + dot(mix_ref[0, at, :], out_ref_w[0])
+        fetch.wait()
+        for cols in chunks(width, 384):
+            acc[:, cols] = acc[:, cols] + dot(peer_ref[...], weight[:, cols])
 
         @pl.loop(0, rows // 16)
         def _(i):
@@ -249,11 +279,9 @@
 
         @pl.when(step == stage)
         def _():
-            @pl.loop(0, 3)
-            def _(i):
-                at = pl.ds(pl.multiple_of(i * tile, 16), tile)
-                proj[part, at, :] = (
-                    dot_nt(normed[at, :], mat_ref[0]).astype(BF16).astype(F32)
+            for cols in chunks(channels):
+                proj[part, :, cols] = (
+                    dot_nt(normed[...], mat_ref[0, cols, :]).astype(BF16).astype(F32)
                 )
 
     @pl.when(step == 2)
@@ -295,8 +323,8 @@
             query_ref[pl.ds(row, 32), :] = short_filter(proj, 0, at, 32, taps)
 
 
-def second_block(tokens, embedding, mixes, weights, gain, matrix, taps, rate):
-    _, rows, channels = mixes.shape
+def second_block(tokens, embedding, mix, peer_mix, weights, peer_weights, gain, matrix, taps, rate):
+    rows, channels = mix.shape
     vocab, width = embedding.shape
     length = rows - LEAD
     modes = rate.shape[0]
@@ -308,8 +336,10 @@
         in_specs=[
             pl.BlockSpec((rows, 1), whole2),
             pl.BlockSpec((vocab, width), whole2),
-            pl.BlockSpec((1, rows, channels), lambda i: (jnp.minimum(i, 1), 0, 0)),
-            pl.BlockSpec((1, channels, width), lambda i: (jnp.minimum(i, 1), 0, 0)),
+            pl.BlockSpec((rows, channels), whole2),
+            pl.BlockSpec((rows, channels), whole2),
+            pl.BlockSpec((channels, width), whole2),
+            pl.BlockSpec(memory_space=pl.ANY),
             pl.BlockSpec((1, width), whole2),
             pl.BlockSpec(
                 (1, channels, width),
@@ -337,9 +367,11 @@
             pltpu.VMEM((rows, width), BF16),
             pltpu.VMEM((3, rows, channels), F32),
             pltpu.VMEM((length, channels), F32),
+            pltpu.VMEM((channels, width), BF16),
+            pltpu.SemaphoreType.DMA,
         ],
         compiler_params=params(),
-    )(tokens[:, None], embedding, mixes, weights, gain[None], matrix, taps, rate)
+    )(tokens[:, None], embedding, mix, peer_mix, weights, peer_weights, gain[None], matrix, taps, rate)
 
 
 def lanes(channels):
@@ -368,21 +400,47 @@
     lax.fori_loop(0, groups, advance, values)
 
 
-def within_kernel(gate_ref, rate_ref, res_ref, skip_ref, fwd_ref, inv_ref, out_ref,
-                  coef, taps, freq, spec, zh, zl):
+def tail_kernel(
+    size, closing_ref, gate_ref, rate_ref, res_ref, skip_ref, fwd_ref, inv_ref, before_ref,
+    query_ref, out_ref, segments, enter, gain, taps, freq, spec, zh, zl, total,
+    send_sem, recv_sem,
+):
+    me = lax.axis_index("context")
+    barrier = pltpu.get_barrier_semaphore()
+    for hop in range(1, size):
+        pl.semaphore_signal(
+            barrier, inc=1, device_id={"context": lax.rem(me + hop, size)}, device_id_type=MESH
+        )
+    segments[me] = closing_ref[...]
     length, channels = gate_ref.shape
     rate = rate_ref[...]
     doubled = 2.0 * rate
-    series = doubled * (1.0 - doubled * (0.5 - doubled * (1.0 / 6.0 - doubled * (1.0 / 24.0 - doubled / 120.0))))
-    coef[...] = res_ref[...] * jnp.sqrt(
+    series = doubled * (
+        1.0
+        - doubled * (0.5 - doubled * (1.0 / 6.0 - doubled * (1.0 / 24.0 - doubled / 120.0)))
+    )
+    gain[...] = res_ref[...] * jnp.sqrt(
         jnp.where(doubled < 0.03, series, 1.0 - jnp.exp(-doubled))
     )
+    pl.semaphore_wait(barrier, size - 1)
+    copies = []
+    for hop in range(1, size):
+        copy = pltpu.make_async_remote_copy(
+            src_ref=closing_ref,
+            dst_ref=segments.at[me],
+            send_sem=send_sem.at[hop],
+            recv_sem=recv_sem.at[hop],
+            device_id={"context": lax.rem(me + hop, size)},
+            device_id_type=MESH,
+        )
+        copy.start()
+        copies.append(copy)
     for lane, width in lanes(channels):
 
         def store(group, rows):
             taps[pl.ds(pl.multiple_of(group * 8, 8), 8), lane : lane + width] = rows
 
-        modal_rows(rate_ref, coef, BLOCK // 8, lane, width, store)
+        modal_rows(rate_ref, gain, BLOCK // 8, lane, width, store)
     freq[...] = forward_wide(fwd_ref, taps[...])
     for b in range(length // BLOCK):
         here = slice(b * BLOCK, (b + 1) * BLOCK)
@@ -397,73 +455,59 @@
             zh[re, :], zl[re, :] = split(u * a - v * c)
             zh[im, :], zl[im, :] = split(u * c + v * a)
 
-        out_ref[here, :] = inverse_wide(inv_ref, zh, zl) + skip_ref[...] * gate_ref[
+        total[here, :] = inverse_wide(inv_ref, zh, zl) + skip_ref[...] * gate_ref[
             here, :
         ].astype(F32)
 
-
-def within_block(gate, rate, residue, skip, fwd, inv):
+    for copy in copies:
+        copy.wait()
+    shard_step = jnp.exp(-rate * float(length))
+    incoming = jnp.zeros(rate.shape, F32)
+    for source in range(size):
+        incoming = jnp.where(
+            source < me, incoming * shard_step + segments[source].astype(F32), incoming
+        )
+    for b in range(length // BLOCK):
+        enter[b] = (
+            gain[...]
+            * jnp.exp(-rate)
+            * (before_ref[b] + jnp.exp(-rate * float(b * BLOCK)) * incoming)
+        )
+    for b in range(length // BLOCK):
+        for lane, width in lanes(channels):
+            cols = slice(lane, lane + width)
+
+            def store(group, rows):
+                at = pl.ds(pl.multiple_of(b * BLOCK + group * 8, 8), 8)
+                total[at, cols] = query_ref[at, cols] * (total[at, cols] + rows)
+
+            modal_rows(rate_ref, enter.at[b], BLOCK // 8, lane, width, store)
+        here = slice(b * BLOCK, (b + 1) * BLOCK)
+        out_ref[here, :] = total[here, :].astype(BF16)
+
+
+def tail_block(size, closing, gate, rate, residue, skip, fwd, inv, before, query):
     length, channels = gate.shape
     return pl.pallas_call(
-        within_kernel,
-        out_shape=jax.ShapeDtypeStruct((length, channels), F32),
+        functools.partial(tail_kernel, size),
+        in_specs=[pl.BlockSpec(memory_space=pltpu.VMEM)] * 9,
+        out_specs=pl.BlockSpec(memory_space=pltpu.VMEM),
+        out_shape=jax.ShapeDtypeStruct((length, channels), BF16),
         scratch_shapes=[
+            pltpu.VMEM((size,) + closing.shape, BF16),
+            pltpu.VMEM(before.shape, F32),
             pltpu.VMEM(rate.shape, F32),
             pltpu.VMEM((BLOCK, channels), F32),
             pltpu.VMEM((2 * BLOCK, channels), F32),
             pltpu.VMEM((2 * BLOCK, channels), F32),
             pltpu.VMEM((2 * BLOCK, channels), BF16),
             pltpu.VMEM((2 * BLOCK, channels), BF16),
-        ],
-        compiler_params=params(),
-        cost_estimate=pl.CostEstimate(
-            flops=8_000_000_000, bytes_accessed=4_000_000, transcendentals=0
-        ),
-    )(gate, rate, residue, skip[None], fwd, inv)
-
-
-def finish_kernel(pos_ref, seg_ref, rate_ref, res_ref, before_ref, query_ref, within_ref,
-                  out_ref, coef):
-    length, channels = query_ref.shape
-    rate = rate_ref[...]
-    shard_step = jnp.exp(-rate * float(length))
-    position = pos_ref[0]
-
-    def gather(source, total):
-        return jnp.where(
-            source < position, total * shard_step + seg_ref[source].astype(F32), total
-        )
-
-    incoming = lax.fori_loop(0, seg_ref.shape[0], gather, jnp.zeros(rate.shape, F32))
-    doubled = 2.0 * rate
-    series = doubled * (1.0 - doubled * (0.5 - doubled * (1.0 / 6.0 - doubled * (1.0 / 24.0 - doubled / 120.0))))
-    gain = res_ref[...] * jnp.sqrt(jnp.where(doubled < 0.03, series, 1.0 - jnp.exp(-doubled)))
-    for b in range(length // BLOCK):
-        coef[b] = (
-            gain * jnp.exp(-rate) * (before_ref[b] + jnp.exp(-rate * float(b * BLOCK)) * incoming)
-        )
-    for b in range(length // BLOCK):
-        for lane, width in lanes(channels):
-            cols = slice(lane, lane + width)
-
-            def store(group, rows):
-                at = pl.ds(pl.multiple_of(b * BLOCK + group * 8, 8), 8)
-                out_ref[at, cols] = query_ref[at, cols] * (within_ref[at, cols] + rows)
-
-            modal_rows(rate_ref, coef.at[b], BLOCK // 8, lane, width, store)
-
-
-def finish_block(position, segments, rate, residue, before, query, within):
-    length, channels = query.shape
-    return pl.pallas_call(
-        finish_kernel,
-        in_specs=[pl.BlockSpec(memory_space=pltpu.SMEM)]
-        + [pl.BlockSpec(memory_space=pltpu.VMEM)] * 6,
-        out_specs=pl.BlockSpec(memory_space=pltpu.VMEM),
-        out_shape=jax.ShapeDtypeStruct((length, channels), F32),
-        scratch_shapes=[pltpu.VMEM(before.shape, F32)],
-        compiler_params=params(),
-    )(position, segments, rate, residue, before, query, within)
+            pltpu.VMEM((length, channels), F32),
+            pltpu.SemaphoreType.DMA((size,)),
+            pltpu.SemaphoreType.DMA((size,)),
+        ],
+        compiler_params=params(1),
+    )(closing, gate, rate, residue, skip[None], fwd, inv, before, query)
 
 
 def on_device(
@@ -476,22 +520,32 @@
     position = lax.axis_index("context")
     side = lax.axis_index("tensor")
     swap = [(0, 1), (1, 0)]
-    all_tokens = lax.all_gather(tokens, ("context", "tensor"), axis=0, tiled=True)
-    weights_a = lax.all_gather(out_proj_a, "tensor", axis=0)
+    size = lax.axis_size("context")
+    both = ("context", "tensor")
+    other_tokens = lax.ppermute(tokens, "tensor", swap)
+    edge = tokens[own_rows - HALO :]
+    halo = sum(
+        lax.ppermute(edge, both, [(2 * c + 1, 2 * c + 2 + t) for c in range(size - 1)])
+        for t in range(2)
+    )
+    weights_a = lax.ppermute(out_proj_a, "tensor", swap)
     weights_b = lax.ppermute(out_proj_b, "tensor", swap)
     table = make_table(embedding, gain_a, in_proj_a)
-    padded = jnp.concatenate([jnp.full((HALO,), -1, jnp.int32), all_tokens])
-    near = lax.dynamic_slice_in_dim(padded, position * length, length + HALO, 0)
-    mixed = medium_mix(near, table, short_a, mr_filter, mr_skip, fwd, inv)
-    mixes = lax.all_gather(mixed, "tensor", axis=0)
+    near = jnp.concatenate(
+        [
+            jnp.where(position == 0, -1, halo),
+            jnp.where(side == 0, tokens, other_tokens),
+            jnp.where(side == 0, other_tokens, tokens),
+        ]
+    )
+    mixed, peer_mixed = medium_mix(near, table, short_a, mr_filter, mr_skip, fwd, inv)
     second, query, gate, before, closing = second_block(
-        near[HALO - LEAD :], embedding, mixes, weights_a, gain_b, in_proj_b, short_b, li_rate
-    )
-    segments = lax.all_gather(closing, "context", axis=0)
-    within = within_block(gate, li_rate, li_residue, li_skip, fwd, inv)
-    mixture = finish_block(
-        position[None], segments, li_rate, li_residue, before, query, within
-    ).astype(BF16)
+        near[HALO - LEAD :], embedding, mixed, peer_mixed, out_proj_a, weights_a, gain_b,
+        in_proj_b, short_b, li_rate,
+    )
+    mixture = tail_block(
+        size, closing, gate, li_rate, li_residue, li_skip, fwd, inv, before, query
+    )
     sent = lax.dynamic_slice_in_dim(mixture, (1 - side) * own_rows, own_rows, 0)
     kept = lax.dynamic_slice_in_dim(mixture, side * own_rows, own_rows, 0)
     other = lax.ppermute(sent, "tensor", swap)

time: 223 us -> 107 us (0.48)
  the two profiles are of different devices: /device:TPU:1 before, /device:TPU:13 now
where the time goes in v1:
time: 107 us; the launch traced here: 106 us
  Pallas kernels  82.9 us (77%)
  starting transfers between devices  8.54 us (8%)
  matrix products  8.02 us (7%)
  local copies, waits for them, and re-layouts  6.57 us (6%)
    pallas_call x1, Pallas kernels, second_block(): pl.pallas_call(second_kernel, grid=(4,), in_specs=[pl.BlockSpec((rows, 1)...  31.1 us
    pallas_call x1, Pallas kernels, tail_block(): pl.pallas_call(functools.partial(tail_kernel, size), in_specs=[pl.BlockSp...  23.5 us
    pallas_call x1, Pallas kernels, medium_mix(): pl.pallas_call(medium_kernel, out_shape=[jax.ShapeDtypeStruct((rows - HAL...  15.4 us
    pallas_call x1, Pallas kernels, make_table(): pl.pallas_call(table_kernel, grid=(parts,), in_specs=[pl.BlockSpec((vocab...  12.9 us
    dot_general x2, matrix products, dot(): return jnp.dot(a, b, preferred_element_type=F32)  8.02 us
    ppermute x2, starting transfers between devices, on_device(): lax.ppermute(edge, both, [(2 * c + 1, 2 * c + 2 + t) for c in range(size...  6.11 us
  transfers between devices with their start and end apart: 6, of which 0 were waited for; matrix products, arithmetic and copies ran while one was open for 10% of the time, Pallas kernels for 78%

profile of v1, /device:TPU:13, one launch (start us, length us, event | category | flops | bytes accessed | tf_op | source)
XLA Modules:
  0.0 106.3 jit_solution(4071161645942108562)
XLA Ops:
  0.0 0.7 collective-permute-start.3
  0.7 0.0 collective-permute-start.5
  0.7 0.5 collective-permute-start.2
  1.2 0.7 slice.6
  1.9 3.0 %collective-permute-start = (s32[160]{0:T(256)S(1)}, s32[160]{0:T(256)S(1)}, u32[]{:S(2)}, u32[]{:S(2)}) collective-permute-start(s32[160]{0:T(256)S(1)} %slice.6), channel_id=1, source_target_pairs={{1,2},{3,4},{5,6},{7,8},{9,10},{11,12},{13,14},{15,16},{17,18},{19... | collective-permute-start | bytes 1928 | tf_op jit(solution)/shard_map/ppermute | solution.py:528
  4.9 3.1 %collective-permute-start.1 = (s32[160]{0:T(256)S(1)}, s32[160]{0:T(256)S(1)}, u32[]{:S(2)}, u32[]{:S(2)}) collective-permute-start(s32[160]{0:T(256)S(1)} %slice.6), channel_id=1, source_target_pairs={{1,3},{3,5},{5,7},{7,9},{9,11},{11,13},{13,15},{15,17},{17,19},{19... | collective-permute-start | bytes 1928 | tf_op jit(solution)/shard_map/ppermute | solution.py:528
  8.1 1.3 %broadcast_in_dim.25.gain_ref = f32[1,1920]{1,0:T(1,128)} reshape(f32[1920]{0:T(1024)} %param.19) | data formatting | bytes 15360 | tf_op jit(solution)/shard_map/broadcast_in_dim | solution.py:132
  9.4 0.0 copy-start
  9.4 0.0 copy-start.1
  9.4 12.9 %shard_map.163.table_ref = bf16[3,512,960]{2,1,0:T(8,128)(2,1)} custom-call(bf16[512,1920]{1,0:T(8,128)(2,1)} %emb_ref.3, f32[1,1920]{1,0:T(1,128)} %broadcast_in_dim.25.gain_ref, bf16[3,960,1920]{2,1,0:T(8,128)(2,1)} %mat_ref.2), custom_call_target="tpu_custom_call" | custom-call | flops 5662310400 | bytes 14008320 | tf_op jit(solution)/shard_map/pallas_call | solution.py:115
  22.3 0.0 copy-done
  22.3 1.0 copy.20.filt_ref
  23.3 0.0 copy-done.1
  23.3 0.6 broadcast_in_dim.27.gain_ref
  23.9 0.0 collective-permute-done
  23.9 0.0 collective-permute-done.1
  23.9 0.0 collective-permute-done.2
  23.9 0.0 copy-done.2
  23.9 0.1 pad_add_fusion
  24.0 0.9 broadcast_in_dim.30.tok_ref
  24.9 0.1 slice.7
  25.0 0.9 broadcast_in_dim.29.tok_ref
  25.8 15.4 %shard_map.164 = (bf16[528,960]{1,0:T(8,128)(2,1)}, bf16[528,960]{1,0:T(8,128)(2,1)}) custom-call(s32[672,1]{1,0:T(8,128)} %broadcast_in_dim.30.tok_ref, bf16[3,512,960]{2,1,0:T(8,128)(2,1)} %shard_map.163.table_ref, f32[3,3,960]{2,1,0:T(4,128)} %taps_ref.2, f32[128,960]{1,0:T(8,128)} %copy.20.filt_ref, f32[1,960]{1,0:T(1,128)} %bitcast.5, ...), custom_call_target="tpu_custom_call" | custom-call | tf_op jit(solution)/shard_map/pallas_call | solution.py:226
  41.3 0.0 collective-permute-done.3.peer_w
  41.3 31.1 %shard_map.165 = (bf16[528,1920]{1,0:T(8,128)(2,1)}, f32[512,960]{1,0:T(8,128)}, bf16[512,960]{1,0:T(8,128)(2,1)}, f32[4,16,960]{2,1,0:T(8,128)}, bf16[16,960]{1,0:T(8,128)(2,1)}) custom-call(s32[528,1]{1,0:T(8,128)} %broadcast_in_dim.29.tok_ref, bf16[512,1920]{1,0:T(8,128)(2,1)} %emb_ref.3, bf16[528,960]{1,0:T(8,128)(2,1)} %get-tuple-element.12.mix_ref, ...), custom_call_target="tpu_custom_call" | custom-call | tf_op jit(solution)/shard_map/pallas_call | solution.py:333
  72.4 23.5 %shard_map.166 = bf16[512,960]{1,0:T(8,128)(2,1)} custom-call(bf16[16,960]{1,0:T(8,128)(2,1)} %get-tuple-element.15.closing_ref, bf16[512,960]{1,0:T(8,128)(2,1)} %get-tuple-element.16.gate_ref, f32[16,960]{1,0:T(8,128)} %rate_ref.3, f32[16,960]{1,0:T(8,128)} %res_ref.1, f32[1,960]{1,0:T(1,128)} %bitcast.6, bf16[256,256]{1,0:T(8,128)(2,1)} %constant.27.clone.fwd_ref, ...), custom_call_target="tpu_custom_call" | custom-call | tf_op jit(solution)/shard_map/pallas_call | solution.py:491
  95.9 1.1 %constant_dynamic-slice_fusion = bf16[256,960]{1,0:T(8,128)(2,1)S(1)} fusion(bf16[512,960]{1,0:T(8,128)(2,1)} %shard_map.166, s32[]{:T(128)S(6)} %select_n.36), kind=kLoop, calls=%fused_computation.7 | loop fusion | bytes 983044 | tf_op jit(solution)/shard_map/dynamic_slice | solution.py:549
  97.0 1.2 %collective-permute-start.4 = (bf16[256,960]{1,0:T(8,128)(2,1)S(1)}, bf16[256,960]{1,0:T(8,128)(2,1)S(1)}, u32[]{:S(2)}, u32[]{:S(2)}) collective-permute-start(bf16[256,960]{1,0:T(8,128)(2,1)S(1)} %constant_dynamic-slice_fusion), channel_id=1, source_target_pairs={{0,1},{1,0},{2,3},{3,2},{4,5},{5,4},{6,7},{7,6},{8,9},{9,8},{10,11... | collective-permute-start | bytes 1474568 | tf_op jit(solution)/shard_map/ppermute | solution.py:551
  98.2 3.5 %fusion = f32[256,1920]{1,0:T(8,128)S(1)} fusion(bf16[960,1920]{1,0:T(8,128)(2,1)} %param.31, bf16[512,960]{1,0:T(8,128)(2,1)} %shard_map.166, s32[]{:T(128)S(6)} %select_n.35), kind=kOutput, calls=%fused_computation.1 | convolution fusion | flops 943718400 | bytes 6176772 | tf_op jit(solution)/shard_map/dot_general | solution.py:56
  101.7 0.0 collective-permute-done.5
  101.7 0.0 collective-permute-done.4
  101.7 4.6 %add_convert_fusion = bf16[256,1920]{1,0:T(8,128)(2,1)} fusion(f32[256,1920]{1,0:T(8,128)S(1)} %fusion, bf16[528,1920]{1,0:T(8,128)(2,1)} %get-tuple-element.14, s32[]{:T(128)S(6)} %select_n.34, bf16[256,960]{1,0:T(8,128)(2,1)S(1)} %collective-permute-done.4, bf16[960,1920]{1,0:T(8,128)(2,1)} %collective-permute-done.5), kind=kOutput, calls=%fused_computation | convolution fusion | flops 945684480 | bytes 8110084 | tf_op jit(solution)/shard_map/dot_general | solution.py:56
  (3 shorter events, 0.0 us)
Async XLA Ops:
  0.0 41.3 %collective-permute-start.3 = (bf16[960,1920]{1,0:T(8,128)(2,1)}, bf16[960,1920]{1,0:T(8,128)(2,1)}, u32[]{:S(2)}, u32[]{:S(2)}) collective-permute-start(bf16[960,1920]{1,0:T(8,128)(2,1)} %own_w.1), channel_id=1, source_target_pairs={{0,1},{1,0},{2,3},{3,2},{4,5},{5,4},{6,7},{7,6},{8,9},{9,8},{10,11... | collective-permute-start | bytes 11059208 | tf_op jit(solution)/shard_map/ppermute | solution.py:531
  0.7 101.0 %collective-permute-start.5 = (bf16[960,1920]{1,0:T(8,128)(2,1)}, bf16[960,1920]{1,0:T(8,128)(2,1)}, u32[]{:S(2)}, u32[]{:S(2)}) collective-permute-start(bf16[960,1920]{1,0:T(8,128)(2,1)} %param.31), channel_id=1, source_target_pairs={{0,1},{1,0},{2,3},{3,2},{4,5},{5,4},{6,7},{7,6},{8,9},{9,8},{10,11... | collective-permute-start | bytes 11059208 | tf_op jit(solution)/shard_map/ppermute | solution.py:532
  0.7 23.2 %collective-permute-start.2 = (s32[256]{0:T(256)}, s32[256]{0:T(256)S(1)}, u32[]{:S(2)}, u32[]{:S(2)}) collective-permute-start(s32[256]{0:T(256)} %param.17), channel_id=1, source_target_pairs={{0,1},{1,0},{2,3},{3,2},{4,5},{5,4},{6,7},{7,6},{8,9},{9,8},{10,11... | collective-permute-start | bytes 3080 | tf_op jit(solution)/shard_map/ppermute | solution.py:525
  1.9 21.9 %collective-permute-start = (s32[160]{0:T(256)S(1)}, s32[160]{0:T(256)S(1)}, u32[]{:S(2)}, u32[]{:S(2)}) collective-permute-start(s32[160]{0:T(256)S(1)} %slice.6), channel_id=1, source_target_pairs={{1,2},{3,4},{5,6},{7,8},{9,10},{11,12},{13,14},{15,16},{17,18},{19... | collective-permute-start | bytes 1928 | tf_op jit(solution)/shard_map/ppermute | solution.py:528
  4.9 18.9 %collective-permute-start.1 = (s32[160]{0:T(256)S(1)}, s32[160]{0:T(256)S(1)}, u32[]{:S(2)}, u32[]{:S(2)}) collective-permute-start(s32[160]{0:T(256)S(1)} %slice.6), channel_id=1, source_target_pairs={{1,3},{3,5},{5,7},{7,9},{9,11},{11,13},{13,15},{15,17},{17,19},{19... | collective-permute-start | bytes 1928 | tf_op jit(solution)/shard_map/ppermute | solution.py:528
  9.4 12.9 %copy-start = (f32[128,960]{0,1:T(8,128)S(1)}, f32[128,960]{0,1:T(8,128)}, u32[]{:S(2)}) copy-start(f32[128,960]{0,1:T(8,128)} %param.22) | copy-start | bytes 1474564
  9.4 13.9 %copy-start.1 = (f32[1920]{0:T(1024)S(1)}, f32[1920]{0:T(1024)}, u32[]{:S(2)}) copy-start(f32[1920]{0:T(1024)} %param.25) | copy-start | bytes 23044
  9.4 14.5 %copy-start.2 = (s32[256]{0:T(256)S(1)}, s32[256]{0:T(256)}, u32[]{:S(2)}) copy-start(s32[256]{0:T(256)} %param.17) | copy-start | bytes 3076
  97.0 4.7 %collective-permute-start.4 = (bf16[256,960]{1,0:T(8,128)(2,1)S(1)}, bf16[256,960]{1,0:T(8,128)(2,1)S(1)}, u32[]{:S(2)}, u32[]{:S(2)}) collective-permute-start(bf16[256,960]{1,0:T(8,128)(2,1)S(1)} %constant_dynamic-slice_fusion), channel_id=1, source_target_pairs={{0,1},{1,0},{2,3},{3,2},{4,5},{5,4},{6,7},{7,6},{8,9},{9,8},{10,11... | collective-permute-start | bytes 1474568 | tf_op jit(solution)/shard_map/ppermute | solution.py:551

commit v2 on v1

--- a/solution.py
+++ b/solution.py
@@ -240,14 +240,28 @@
             pltpu.SemaphoreType.DMA(((rows - HALO) // BLOCK,)),
         ],
         compiler_params=params(0),
-    )(tokens[:, None], table, taps, filt, skip[None], fwd, inv)
+    )(tokens, table, taps, filt, skip[None], fwd, inv)
 
 
 def second_kernel(
-    tok_ref, emb_ref, mix_ref, peer_ref, own_w, peer_w, gain_ref, mat_ref, taps_ref, rate_ref,
-    second_ref, query_ref, gate_ref, before_ref, closing_ref,
-    acc, normed, proj, gate_f, weight, weight_sem,
+    size, tok_ref, emb_ref, mix_ref, peer_ref, own_w, peer_w, gain_ref, mat_ref, taps_ref, rate_ref,
+    res_ref, skip_ref, fwd_ref, inv_ref, second_ref, mixture_ref,
+    acc, normed, proj, gate_f, weight, weight_sem, gate_ref, before_ref, closing_ref,
+    segments, enter, gain, kernel, freq, spec, zh, zl, send_sem, recv_sem,
 ):
+    me = lax.axis_index("context")
+    barrier = pltpu.get_barrier_semaphore()
+    copies = [
+        pltpu.make_async_remote_copy(
+            src_ref=closing_ref,
+            dst_ref=segments.at[me],
+            send_sem=send_sem.at[hop],
+            recv_sem=recv_sem.at[hop],
+            device_id={"context": lax.rem(me + hop, size)},
+            device_id_type=MESH,
+        )
+        for hop in range(1, size)
+    ]
     step = pl.program_id(0)
     rows, width = acc.shape
     vocab = emb_ref.shape[0]
@@ -258,7 +272,11 @@
     @pl.when(step == 0)
     def _():
         fetch.start()
-        picked = onehot(tok_ref[...], vocab)
+        for hop in range(1, size):
+            pl.semaphore_signal(
+                barrier, inc=1, device_id={"context": lax.rem(me + hop, size)}, device_id_type=MESH
+            )
+        picked = onehot(tok_ref[HALO - LEAD :, :], vocab)
         for cols in chunks(width, 384):
             acc[:, cols] = dot(picked, emb_ref[:, cols]) + dot(mix_ref[...], own_w[:, cols])
 
@@ -311,6 +329,10 @@
 
             state = lax.fori_loop(0, BLOCK // 8, advance, state)
         closing_ref[...] = state.astype(BF16)
+        segments[me] = closing_ref[...]
+        pl.semaphore_wait(barrier, size - 1)
+        for copy in copies:
+            copy.start()
 
     @pl.when(step == 3)
     def _():
@@ -320,25 +342,85 @@
         def _(i):
             row = pl.multiple_of(i * 32, 32)
             at = pl.multiple_of(row + LEAD - 8, 8)
-            query_ref[pl.ds(row, 32), :] = short_filter(proj, 0, at, 32, taps)
-
-
-def second_block(tokens, embedding, mix, peer_mix, weights, peer_weights, gain, matrix, taps, rate):
+            proj[1, pl.ds(row, 32), :] = short_filter(proj, 0, at, 32, taps)
+
+        rate = rate_ref[...]
+        doubled = 2.0 * rate
+        series = doubled * (
+            1.0
+            - doubled * (0.5 - doubled * (1.0 / 6.0 - doubled * (1.0 / 24.0 - doubled / 120.0)))
+        )
+        gain[...] = res_ref[...] * jnp.sqrt(
+            jnp.where(doubled < 0.03, series, 1.0 - jnp.exp(-doubled))
+        )
+        for lane, span in lanes(channels):
+
+            def store(group, rows):
+                kernel[pl.ds(pl.multiple_of(group * 8, 8), 8), lane : lane + span] = rows
+
+            modal_rows(rate_ref, gain, BLOCK // 8, lane, span, store)
+        freq[...] = forward_wide(fwd_ref, kernel[...])
+        for b in range(length // BLOCK):
+            here = slice(b * BLOCK, (b + 1) * BLOCK)
+            spec[...] = forward_exact(fwd_ref, gate_ref[here, :])
+
+            @pl.loop(0, BLOCK // 32)
+            def _(i):
+                re = pl.ds(pl.multiple_of(i * 32, 32), 32)
+                im = pl.ds(pl.multiple_of(BLOCK + i * 32, 32), 32)
+                u, v = spec[re, :], spec[im, :]
+                a, c = freq[re, :], freq[im, :]
+                zh[re, :], zl[re, :] = split(u * a - v * c)
+                zh[im, :], zl[im, :] = split(u * c + v * a)
+
+            acc[here, :channels] = inverse_wide(inv_ref, zh, zl) + skip_ref[...] * gate_ref[
+                here, :
+            ].astype(F32)
+
+        for copy in copies:
+            copy.wait()
+        shard_step = jnp.exp(-rate * float(length))
+        incoming = jnp.zeros(rate.shape, F32)
+        for source in range(size):
+            incoming = jnp.where(
+                source < me, incoming * shard_step + segments[source].astype(F32), incoming
+            )
+        for b in range(length // BLOCK):
+            enter[b] = (
+                gain[...]
+                * jnp.exp(-rate)
+                * (before_ref[b] + jnp.exp(-rate * float(b * BLOCK)) * incoming)
+            )
+        for b in range(length // BLOCK):
+            for lane, span in lanes(channels):
+                cols = slice(lane, lane + span)
+
+                def store(group, rows):
+                    at = pl.ds(pl.multiple_of(b * BLOCK + group * 8, 8), 8)
+                    acc[at, cols] = proj[1, at, cols] * (acc[at, cols] + rows)
+
+                modal_rows(rate_ref, enter.at[b], BLOCK // 8, lane, span, store)
+            here = slice(b * BLOCK, (b + 1) * BLOCK)
+            mixture_ref[here, :] = acc[here, :channels].astype(BF16)
+
+
+def second_block(size, residue, skip, fwd, inv, tokens, embedding, mix, peer_mix, weights, peer_weights, gain, matrix, taps, rate):
     rows, channels = mix.shape
     vocab, width = embedding.shape
     length = rows - LEAD
     modes = rate.shape[0]
     whole2 = lambda i: (0, 0)
     whole3 = lambda i: (0, 0, 0)
+    once = dict(pipeline_mode=pl.Buffered(1))
     return pl.pallas_call(
-        second_kernel,
+        functools.partial(second_kernel, size),
         grid=(4,),
         in_specs=[
-            pl.BlockSpec((rows, 1), whole2),
-            pl.BlockSpec((vocab, width), whole2),
-            pl.BlockSpec((rows, channels), whole2),
-            pl.BlockSpec((rows, channels), whole2),
-            pl.BlockSpec((channels, width), whole2),
+            pl.BlockSpec(tokens.shape, whole2),
+            pl.BlockSpec((vocab, width), whole2, **once),
+            pl.BlockSpec((rows, channels), whole2, **once),
+            pl.BlockSpec((rows, channels), whole2, **once),
+            pl.BlockSpec((channels, width), whole2, **once),
             pl.BlockSpec(memory_space=pl.ANY),
             pl.BlockSpec((1, width), whole2),
             pl.BlockSpec(
@@ -347,20 +429,18 @@
             ),
             pl.BlockSpec(taps.shape, whole3),
             pl.BlockSpec(rate.shape, whole2),
+            pl.BlockSpec(rate.shape, whole2),
+            pl.BlockSpec((1, channels), whole2),
+            pl.BlockSpec(fwd.shape, whole2),
+            pl.BlockSpec(inv.shape, whole2),
         ],
         out_specs=[
             pl.BlockSpec((rows, width), whole2),
             pl.BlockSpec((length, channels), whole2),
-            pl.BlockSpec((length, channels), whole2),
-            pl.BlockSpec((length // BLOCK, modes, channels), whole3),
-            pl.BlockSpec((modes, channels), whole2),
         ],
         out_shape=[
             jax.ShapeDtypeStruct((rows, width), BF16),
-            jax.ShapeDtypeStruct((length, channels), F32),
             jax.ShapeDtypeStruct((length, channels), BF16),
-            jax.ShapeDtypeStruct((length // BLOCK, modes, channels), F32),
-            jax.ShapeDtypeStruct((modes, channels), BF16),
         ],
         scratch_shapes=[
             pltpu.VMEM((rows, width), F32),
@@ -369,9 +449,25 @@
             pltpu.VMEM((length, channels), F32),
             pltpu.VMEM((channels, width), BF16),
             pltpu.SemaphoreType.DMA,
+            pltpu.VMEM((length, channels), BF16),
+            pltpu.VMEM((length // BLOCK, modes, channels), F32),
+            pltpu.VMEM((modes, channels), BF16),
+            pltpu.VMEM((size, modes, channels), BF16),
+            pltpu.VMEM((length // BLOCK, modes, channels), F32),
+            pltpu.VMEM((modes, channels), F32),
+            pltpu.VMEM((BLOCK, channels), F32),
+            pltpu.VMEM((2 * BLOCK, channels), F32),
+            pltpu.VMEM((2 * BLOCK, channels), F32),
+            pltpu.VMEM((2 * BLOCK, channels), BF16),
+            pltpu.VMEM((2 * BLOCK, channels), BF16),
+            pltpu.SemaphoreType.DMA((size,)),
+            pltpu.SemaphoreType.DMA((size,)),
         ],
-        compiler_params=params(),
-    )(tokens[:, None], embedding, mix, peer_mix, weights, peer_weights, gain[None], matrix, taps, rate)
+        compiler_params=params(1),
+    )(
+        tokens, embedding, mix, peer_mix, weights, peer_weights, gain[None], matrix, taps, rate,
+        residue, skip[None], fwd, inv,
+    )
 
 
 def lanes(channels):
@@ -398,116 +494,6 @@
         return [v * s for v, s in zip(values, steps)]
 
     lax.fori_loop(0, groups, advance, values)
-
-
-def tail_kernel(
-    size, closing_ref, gate_ref, rate_ref, res_ref, skip_ref, fwd_ref, inv_ref, before_ref,
-    query_ref, out_ref, segments, enter, gain, taps, freq, spec, zh, zl, total,
-    send_sem, recv_sem,
-):
-    me = lax.axis_index("context")
-    barrier = pltpu.get_barrier_semaphore()
-    for hop in range(1, size):
-        pl.semaphore_signal(
-            barrier, inc=1, device_id={"context": lax.rem(me + hop, size)}, device_id_type=MESH
-        )
-    segments[me] = closing_ref[...]
-    length, channels = gate_ref.shape
-    rate = rate_ref[...]
-    doubled = 2.0 * rate
-    series = doubled * (
-        1.0
-        - doubled * (0.5 - doubled * (1.0 / 6.0 - doubled * (1.0 / 24.0 - doubled / 120.0)))
-    )
-    gain[...] = res_ref[...] * jnp.sqrt(
-        jnp.where(doubled < 0.03, series, 1.0 - jnp.exp(-doubled))
-    )
-    pl.semaphore_wait(barrier, size - 1)
-    copies = []
-    for hop in range(1, size):
-        copy = pltpu.make_async_remote_copy(
-            src_ref=closing_ref,
-            dst_ref=segments.at[me],
-            send_sem=send_sem.at[hop],
-            recv_sem=recv_sem.at[hop],
-            device_id={"context": lax.rem(me + hop, size)},
-            device_id_type=MESH,
-        )
-        copy.start()
-        copies.append(copy)
-    for lane, width in lanes(channels):
-
-        def store(group, rows):
-            taps[pl.ds(pl.multiple_of(group * 8, 8), 8), lane : lane + width] = rows
-
-        modal_rows(rate_ref, gain, BLOCK // 8, lane, width, store)
-    freq[...] = forward_wide(fwd_ref, taps[...])
-    for b in range(length // BLOCK):
-        here = slice(b * BLOCK, (b + 1) * BLOCK)
-        spec[...] = forward_exact(fwd_ref, gate_ref[here, :])
-
-        @pl.loop(0, BLOCK // 32)
-        def _(i):
-            re = pl.ds(pl.multiple_of(i * 32, 32), 32)
-            im = pl.ds(pl.multiple_of(BLOCK + i * 32, 32), 32)
-            u, v = spec[re, :], spec[im, :]
-            a, c = freq[re, :], freq[im, :]
-            zh[re, :], zl[re, :] = split(u * a - v * c)
-            zh[im, :], zl[im, :] = split(u * c + v * a)
-
-        total[here, :] = inverse_wide(inv_ref, zh, zl) + skip_ref[...] * gate_ref[
-            here, :
-        ].astype(F32)
-
-    for copy in copies:
-        copy.wait()
-    shard_step = jnp.exp(-rate * float(length))
-    incoming = jnp.zeros(rate.shape, F32)
-    for source in range(size):
-        incoming = jnp.where(
-            source < me, incoming * shard_step + segments[source].astype(F32), incoming
-        )
-    for b in range(length // BLOCK):
-        enter[b] = (
-            gain[...]
-            * jnp.exp(-rate)
-            * (before_ref[b] + jnp.exp(-rate * float(b * BLOCK)) * incoming)
-        )
-    for b in range(length // BLOCK):
-        for lane, width in lanes(channels):
-            cols = slice(lane, lane + width)
-
-            def store(group, rows):
-                at = pl.ds(pl.multiple_of(b * BLOCK + group * 8, 8), 8)
-                total[at, cols] = query_ref[at, cols] * (total[at, cols] + rows)
-
-            modal_rows(rate_ref, enter.at[b], BLOCK // 8, lane, width, store)
-        here = slice(b * BLOCK, (b + 1) * BLOCK)
-        out_ref[here, :] = total[here, :].astype(BF16)
-
-
-def tail_block(size, closing, gate, rate, residue, skip, fwd, inv, before, query):
-    length, channels = gate.shape
-    return pl.pallas_call(
-        functools.partial(tail_kernel, size),
-        in_specs=[pl.BlockSpec(memory_space=pltpu.VMEM)] * 9,
-        out_specs=pl.BlockSpec(memory_space=pltpu.VMEM),
-        out_shape=jax.ShapeDtypeStruct((length, channels), BF16),
-        scratch_shapes=[
-            pltpu.VMEM((size,) + closing.shape, BF16),
-            pltpu.VMEM(before.shape, F32),
-            pltpu.VMEM(rate.shape, F32),
-            pltpu.VMEM((BLOCK, channels), F32),
-            pltpu.VMEM((2 * BLOCK, channels), F32),
-            pltpu.VMEM((2 * BLOCK, channels), F32),
-            pltpu.VMEM((2 * BLOCK, channels), BF16),
-            pltpu.VMEM((2 * BLOCK, channels), BF16),
-            pltpu.VMEM((length, channels), F32),
-            pltpu.SemaphoreType.DMA((size,)),
-            pltpu.SemaphoreType.DMA((size,)),
-        ],
-        compiler_params=params(1),
-    )(closing, gate, rate, residue, skip[None], fwd, inv, before, query)
 
 
 def on_device(
@@ -538,13 +524,10 @@
             jnp.where(side == 0, other_tokens, tokens),
         ]
     )
-    mixed, peer_mixed = medium_mix(near, table, short_a, mr_filter, mr_skip, fwd, inv)
-    second, query, gate, before, closing = second_block(
-        near[HALO - LEAD :], embedding, mixed, peer_mixed, out_proj_a, weights_a, gain_b,
-        in_proj_b, short_b, li_rate,
-    )
-    mixture = tail_block(
-        size, closing, gate, li_rate, li_residue, li_skip, fwd, inv, before, query
+    mixed, peer_mixed = medium_mix(near[:, None], table, short_a, mr_filter, mr_skip, fwd, inv)
+    second, mixture = second_block(
+        size, li_residue, li_skip, fwd, inv, near[:, None], embedding, mixed, peer_mixed,
+        out_proj_a, weights_a, gain_b, in_proj_b, short_b, li_rate,
     )
     sent = lax.dynamic_slice_in_dim(mixture, (1 - side) * own_rows, own_rows, 0)
     kept = lax.dynamic_slice_in_dim(mixture, side * own_rows, own_rows, 0)

time: 107 us -> 96.8 us (0.905)
  Pallas kernels: 82.9 us -> 73.7 us
    pallas_call x2 -> x1, Pallas kernels: 54.6 us -> 45.5 us  [second_block(): pl.pallas_call(functools.partial(second_kernel, size), grid=(4,), in_spec...]
  transfers between devices with their start and end apart: 6 -> 6, of which waited for: 0 -> 0; matrix products, arithmetic and copies ran while one was open for 10% -> 10% of each run, Pallas kernels for 78% -> 76%
where the time goes in v2:
time: 96.8 us; the launch traced here: 96.5 us
  Pallas kernels  73.7 us (76%)
  starting transfers between devices  8.87 us (9%)
  matrix products  8.02 us (8%)
  local copies, waits for them, and re-layouts  5.65 us (6%)
    pallas_call x1, Pallas kernels, second_block(): pl.pallas_call(functools.partial(second_kernel, size), grid=(4,), in_spec...  45.5 us
    pallas_call x1, Pallas kernels, medium_mix(): pl.pallas_call(medium_kernel, out_shape=[jax.ShapeDtypeStruct((rows - HAL...  15.3 us
    pallas_call x1, Pallas kernels, make_table(): pl.pallas_call(table_kernel, grid=(parts,), in_specs=[pl.BlockSpec((vocab...  12.9 us
    dot_general x2, matrix products, dot(): return jnp.dot(a, b, preferred_element_type=F32)  8.02 us
    ppermute x2, starting transfers between devices, on_device(): lax.ppermute(edge, both, [(2 * c + 1, 2 * c + 2 + t) for c in range(size...  6.11 us
  transfers between devices with their start and end apart: 6, of which 0 were waited for; matrix products, arithmetic and copies ran while one was open for 10% of the time, Pallas kernels for 76%

profile of v2, /device:TPU:13, one launch (start us, length us, event | category | flops | bytes accessed | tf_op | source)
XLA Modules:
  0.0 96.5 jit_solution(13851675174019732551)
XLA Ops:
  0.0 0.7 collective-permute-start.3
  0.7 0.0 collective-permute-start.5
  0.7 0.5 collective-permute-start.2
  1.2 0.7 slice.3
  1.9 3.0 %collective-permute-start = (s32[160]{0:T(256)S(1)}, s32[160]{0:T(256)S(1)}, u32[]{:S(2)}, u32[]{:S(2)}) collective-permute-start(s32[160]{0:T(256)S(1)} %slice.3), channel_id=1, source_target_pairs={{1,2},{3,4},{5,6},{7,8},{9,10},{11,12},{13,14},{15,16},{17,18},{19... | collective-permute-start | bytes 1928 | tf_op jit(solution)/shard_map/ppermute | solution.py:514
  4.9 3.1 %collective-permute-start.1 = (s32[160]{0:T(256)S(1)}, s32[160]{0:T(256)S(1)}, u32[]{:S(2)}, u32[]{:S(2)}) collective-permute-start(s32[160]{0:T(256)S(1)} %slice.3), channel_id=1, source_target_pairs={{1,3},{3,5},{5,7},{7,9},{9,11},{11,13},{13,15},{15,17},{17,19},{19... | collective-permute-start | bytes 1928 | tf_op jit(solution)/shard_map/ppermute | solution.py:514
  8.1 1.3 %broadcast_in_dim.22.gain_ref = f32[1,1920]{1,0:T(1,128)} reshape(f32[1920]{0:T(1024)} %param.19) | data formatting | bytes 15360 | tf_op jit(solution)/shard_map/broadcast_in_dim | solution.py:132
  9.4 0.0 copy-start
  9.4 0.0 copy-start.1
  9.4 0.0 copy-start.2
  9.4 12.9 %shard_map.163.table_ref = bf16[3,512,960]{2,1,0:T(8,128)(2,1)} custom-call(bf16[512,1920]{1,0:T(8,128)(2,1)} %emb_ref.3, f32[1,1920]{1,0:T(1,128)} %broadcast_in_dim.22.gain_ref, bf16[3,960,1920]{2,1,0:T(8,128)(2,1)} %mat_ref.2), custom_call_target="tpu_custom_call" | custom-call | flops 5662310400 | bytes 14008320 | tf_op jit(solution)/shard_map/pallas_call | solution.py:115
  22.3 0.0 copy-done
  22.3 1.0 %copy.20.filt_ref = f32[128,960]{1,0:T(8,128)} copy(f32[128,960]{0,1:T(8,128)S(1)} %copy-done) | data formatting | bytes 983040 | tf_op args[5]
  23.3 0.0 copy-done.1
  23.3 0.6 broadcast_in_dim.24.gain_ref
  23.9 0.0 collective-permute-done
  23.9 0.0 collective-permute-done.1
  23.9 0.0 collective-permute-done.2
  23.9 0.0 copy-done.2
  23.9 0.1 pad_add_fusion
  24.0 0.9 broadcast_in_dim.26.tok_ref
  24.9 15.3 %shard_map.164 = (bf16[528,960]{1,0:T(8,128)(2,1)}, bf16[528,960]{1,0:T(8,128)(2,1)}) custom-call(s32[672,1]{1,0:T(8,128)} %broadcast_in_dim.26.tok_ref, bf16[3,512,960]{2,1,0:T(8,128)(2,1)} %shard_map.163.table_ref, f32[3,3,960]{2,1,0:T(4,128)} %taps_ref.2, f32[128,960]{1,0:T(8,128)} %copy.20.filt_ref, f32[1,960]{1,0:T(1,128)} %bitcast.5, ...), custom_call_target="tpu_custom_call" | custom-call | tf_op jit(solution)/shard_map/pallas_call | solution.py:226
  40.2 0.0 collective-permute-done.3.peer_w
  40.3 45.5 %shard_map.165 = (bf16[528,1920]{1,0:T(8,128)(2,1)}, bf16[512,960]{1,0:T(8,128)(2,1)}) custom-call(s32[672,1]{1,0:T(8,128)} %broadcast_in_dim.26.tok_ref, bf16[512,1920]{1,0:T(8,128)(2,1)} %emb_ref.3, bf16[528,960]{1,0:T(8,128)(2,1)} %get-tuple-element.9.mix_ref, bf16[528,960]{1,0:T(8,128)(2,1)} %get-tuple-element.10.peer_ref, bf16[960,1920]{1,0:T(8,128)(2,1)} %own_w.1, ...), custom_call_target="tpu_custom_call" | custom-call | tf_op jit(solution)/shard_map/pallas_call | solution.py:415
  85.8 1.1 %constant_dynamic-slice_fusion = bf16[256,960]{1,0:T(8,128)(2,1)S(1)} fusion(bf16[512,960]{1,0:T(8,128)(2,1)} %get-tuple-element.12, s32[]{:T(128)S(6)} %select_n.36), kind=kLoop, calls=%fused_computation.7 | loop fusion | bytes 983044 | tf_op jit(solution)/shard_map/dynamic_slice | solution.py:532
  86.9 1.6 %collective-permute-start.4 = (bf16[256,960]{1,0:T(8,128)(2,1)S(1)}, bf16[256,960]{1,0:T(8,128)(2,1)S(1)}, u32[]{:S(2)}, u32[]{:S(2)}) collective-permute-start(bf16[256,960]{1,0:T(8,128)(2,1)S(1)} %constant_dynamic-slice_fusion), channel_id=1, source_target_pairs={{0,1},{1,0},{2,3},{3,2},{4,5},{5,4},{6,7},{7,6},{8,9},{9,8},{10,11... | collective-permute-start | bytes 1474568 | tf_op jit(solution)/shard_map/ppermute | solution.py:534
  88.4 3.5 %fusion = f32[256,1920]{1,0:T(8,128)S(1)} fusion(bf16[960,1920]{1,0:T(8,128)(2,1)} %param.31, bf16[512,960]{1,0:T(8,128)(2,1)} %get-tuple-element.12, s32[]{:T(128)S(6)} %select_n.35), kind=kOutput, calls=%fused_computation.1 | convolution fusion | flops 943718400 | bytes 6176772 | tf_op jit(solution)/shard_map/dot_general | solution.py:56
  91.9 0.0 collective-permute-done.5
  91.9 0.0 collective-permute-done.4
  91.9 4.6 %add_convert_fusion = bf16[256,1920]{1,0:T(8,128)(2,1)} fusion(f32[256,1920]{1,0:T(8,128)S(1)} %fusion, bf16[528,1920]{1,0:T(8,128)(2,1)} %get-tuple-element.11, s32[]{:T(128)S(6)} %select_n.34, bf16[256,960]{1,0:T(8,128)(2,1)S(1)} %collective-permute-done.4, bf16[960,1920]{1,0:T(8,128)(2,1)} %collective-permute-done.5), kind=kOutput, calls=%fused_computation | convolution fusion | flops 945684480 | bytes 8110084 | tf_op jit(solution)/shard_map/dot_general | solution.py:56
  (2 shorter events, 0.0 us)
Async XLA Ops:
  0.0 40.2 %collective-permute-start.3 = (bf16[960,1920]{1,0:T(8,128)(2,1)}, bf16[960,1920]{1,0:T(8,128)(2,1)}, u32[]{:S(2)}, u32[]{:S(2)}) collective-permute-start(bf16[960,1920]{1,0:T(8,128)(2,1)} %own_w.1), channel_id=1, source_target_pairs={{0,1},{1,0},{2,3},{3,2},{4,5},{5,4},{6,7},{7,6},{8,9},{9,8},{10,11... | collective-permute-start | bytes 11059208 | tf_op jit(solution)/shard_map/ppermute | solution.py:517
  0.7 91.2 %collective-permute-start.5 = (bf16[960,1920]{1,0:T(8,128)(2,1)}, bf16[960,1920]{1,0:T(8,128)(2,1)}, u32[]{:S(2)}, u32[]{:S(2)}) collective-permute-start(bf16[960,1920]{1,0:T(8,128)(2,1)} %param.31), channel_id=1, source_target_pairs={{0,1},{1,0},{2,3},{3,2},{4,5},{5,4},{6,7},{7,6},{8,9},{9,8},{10,11... | collective-permute-start | bytes 11059208 | tf_op jit(solution)/shard_map/ppermute | solution.py:518
  0.7 23.2 %collective-permute-start.2 = (s32[256]{0:T(256)}, s32[256]{0:T(256)S(1)}, u32[]{:S(2)}, u32[]{:S(2)}) collective-permute-start(s32[256]{0:T(256)} %param.17), channel_id=1, source_target_pairs={{0,1},{1,0},{2,3},{3,2},{4,5},{5,4},{6,7},{7,6},{8,9},{9,8},{10,11... | collective-permute-start | bytes 3080 | tf_op jit(solution)/shard_map/ppermute | solution.py:511
  1.9 21.9 %collective-permute-start = (s32[160]{0:T(256)S(1)}, s32[160]{0:T(256)S(1)}, u32[]{:S(2)}, u32[]{:S(2)}) collective-permute-start(s32[160]{0:T(256)S(1)} %slice.3), channel_id=1, source_target_pairs={{1,2},{3,4},{5,6},{7,8},{9,10},{11,12},{13,14},{15,16},{17,18},{19... | collective-permute-start | bytes 1928 | tf_op jit(solution)/shard_map/ppermute | solution.py:514
  4.9 18.9 %collective-permute-start.1 = (s32[160]{0:T(256)S(1)}, s32[160]{0:T(256)S(1)}, u32[]{:S(2)}, u32[]{:S(2)}) collective-permute-start(s32[160]{0:T(256)S(1)} %slice.3), channel_id=1, source_target_pairs={{1,3},{3,5},{5,7},{7,9},{9,11},{11,13},{13,15},{15,17},{17,19},{19... | collective-permute-start | bytes 1928 | tf_op jit(solution)/shard_map/ppermute | solution.py:514
  9.4 12.9 %copy-start = (f32[128,960]{0,1:T(8,128)S(1)}, f32[128,960]{0,1:T(8,128)}, u32[]{:S(2)}) copy-start(f32[128,960]{0,1:T(8,128)} %param.22) | copy-start | bytes 1474564
  9.4 13.9 %copy-start.1 = (f32[1920]{0:T(1024)S(1)}, f32[1920]{0:T(1024)}, u32[]{:S(2)}) copy-start(f32[1920]{0:T(1024)} %param.25) | copy-start | bytes 23044
  9.4 14.5 %copy-start.2 = (s32[256]{0:T(256)S(1)}, s32[256]{0:T(256)}, u32[]{:S(2)}) copy-start(s32[256]{0:T(256)} %param.17) | copy-start | bytes 3076
  86.9 5.0 %collective-permute-start.4 = (bf16[256,960]{1,0:T(8,128)(2,1)S(1)}, bf16[256,960]{1,0:T(8,128)(2,1)S(1)}, u32[]{:S(2)}, u32[]{:S(2)}) collective-permute-start(bf16[256,960]{1,0:T(8,128)(2,1)S(1)} %constant_dynamic-slice_fusion), channel_id=1, source_target_pairs={{0,1},{1,0},{2,3},{3,2},{4,5},{5,4},{6,7},{7,6},{8,9},{9,8},{10,11... | collective-permute-start | bytes 1474568 | tf_op jit(solution)/shard_map/ppermute | solution.py:534
